TPU v7x, 32 devices: a whole 2x2x4 slice. The times are simulated.
32 devices in a mesh: groups: 2 (over x), traj: 16 (over z, y, core).
Axes of the slice: x: 2, y: 2, z: 4, core: 2. Of those that a mesh axis runs over, the one named last changes fastest.
Arguments:
- lengths: int32 [8], P('groups'), parts along dimension 0, may hold values from 1 to 4096, 8192 in all
- pattern: int32 [8, 8], replicated, may hold values from 0 to 31, as said below
- first_blocks: bfloat16 [8192, 128], replicated, may hold values from -0.1875 to 0.1875
- second_weight: bfloat16 [1024, 512], replicated, may hold values from -0.1875 to 0.1875
- frames: bfloat16 [16384, 4096], P(('groups', 'traj')), parts along dimension 0, may hold values from -14 to 14
- frame_ok: int32 [16384], P(('groups', 'traj')), parts along dimension 0, may hold values 0 or 1
Outputs:
- score: float32 [2], P('groups'), parts along dimension 0
- grad_first: float32 [16384, 128], P(('groups', 'traj')), parts along dimension 0
- grad_second: float32 [2048, 512], P(('groups', 'traj')), parts along dimension 0
There are 2 independent parts, one for each index of `groups`. A program takes and returns all parts, laid end to end along the dimension named above; an argument that names none is the same for every part. Nothing has to cross between parts.
Inputs may be any that keep to these rules, and one draw needn't show every extreme that they name: `lengths`: the longest trajectory has exactly 4096 frames. `pattern`: indices are distinct within a column block and every row block appears somewhere.
All inputs are finite; a program needn't handle non-finite values. No bound on the sum of `frame_ok` on one device may be relied on, other than what follows from the above.
Results may differ from a plain program's by a relative error of at most 0.013.
Values may be sent and summed in bfloat16 or wider, within the bound.
A program may use at most 128 MiB of HBM per device.

v0:
```python
import jax
import jax.numpy as jnp
from jax import lax
from jax.sharding import PartitionSpec as P

BLK = 128
LAG = 64


EPS = 0.01


def from_behind(block, axis, distance):
    devices = range(lax.axis_size(axis))
    route = [(i - distance, i) for i in devices if i - distance in devices]
    return lax.ppermute(block, axis, route)


def vamp_score(weight_sum, sum_a, sum_b, mom_aa, mom_ab, mom_bb):
    mean_a = sum_a / weight_sum
    mean_b = sum_b / weight_sum
    identity = jnp.eye(mom_aa.shape[0], dtype=mom_aa.dtype)
    cov_aa = mom_aa / weight_sum - jnp.outer(mean_a, mean_a) + EPS * identity
    cov_bb = mom_bb / weight_sum - jnp.outer(mean_b, mean_b) + EPS * identity
    cov_ab = mom_ab / weight_sum - jnp.outer(mean_a, mean_b)
    factor_a = jnp.linalg.cholesky(cov_aa)
    factor_b = jnp.linalg.cholesky(cov_bb)
    partial_solve = jax.scipy.linalg.solve_triangular(factor_a, cov_ab, lower=True)
    whitened = jax.scipy.linalg.solve_triangular(factor_b, partial_solve.T, lower=True)
    return jnp.sum(whitened * whitened) / mom_aa.shape[0]


def pair_weights(lengths, ok_now, ok_lagged, offset):
    positions = offset + jnp.arange(ok_now.shape[0], dtype=jnp.int32)
    bounds = jnp.cumsum(lengths)
    owner_now = jnp.sum((bounds[None, :] <= positions[:, None]).astype(jnp.int32), axis=1)
    owner_lag = jnp.sum((bounds[None, :] <= (positions + LAG)[:, None]).astype(jnp.int32), axis=1)
    keep = (owner_now == owner_lag) & (ok_now > 0.5) & (ok_lagged > 0.5)
    return keep.astype(jnp.float32)


def pick_blocks(rows, pattern):
    split_rows = rows.reshape(rows.shape[0], rows.shape[1] // BLK, BLK)
    return split_rows[:, pattern]


def encode(rows, pattern, first_blocks, second_weight):
    picked = pick_blocks(rows, pattern)
    blocks = first_blocks.reshape(pattern.shape[0], pattern.shape[1], BLK, BLK)
    pre = jnp.einsum("rckb,ckbd->rcd", picked, blocks, preferred_element_type=jnp.float32)
    squash = jnp.tanh(pre.reshape(rows.shape[0], -1))
    hidden = squash.astype(jnp.bfloat16)
    codes = jnp.dot(hidden, second_weight, preferred_element_type=jnp.float32)
    return (picked, squash, hidden, codes)


def moments(weights, codes_a, codes_b):
    highest = lax.Precision.HIGHEST
    contract = (((0,), (0,)), ((), ()))
    scaled_a = codes_a * weights[:, None]
    scaled_b = codes_b * weights[:, None]
    return (
        jnp.sum(weights),
        jnp.sum(scaled_a, axis=0),
        jnp.sum(scaled_b, axis=0),
        lax.dot_general(scaled_a, codes_a, contract, precision=highest),
        lax.dot_general(scaled_a, codes_b, contract, precision=highest),
        lax.dot_general(scaled_b, codes_b, contract, precision=highest),
    )


def code_cotangents(weights, codes_a, codes_b, grads):
    highest = lax.Precision.HIGHEST
    g_sa, g_sb, g_aa, g_ab, g_bb = (grads[1], grads[2], grads[3], grads[4], grads[5])
    cot_a = weights[:, None] * (
        g_sa[None, :]
        + jnp.dot(codes_a, g_aa + g_aa.T, precision=highest)
        + jnp.dot(codes_b, g_ab.T, precision=highest)
    )
    cot_b = weights[:, None] * (
        g_sb[None, :]
        + jnp.dot(codes_b, g_bb + g_bb.T, precision=highest)
        + jnp.dot(codes_a, g_ab, precision=highest)
    )
    return (cot_a.astype(jnp.bfloat16), cot_b.astype(jnp.bfloat16))


def role_terms(picked, squash, hidden, cotan, second_weight):
    back_hidden = lax.dot_general(
        cotan, second_weight, (((1,), (1,)), ((), ())), preferred_element_type=jnp.float32
    )
    back_pre = (back_hidden * (1.0 - squash * squash)).astype(jnp.bfloat16)
    grad_second = lax.dot_general(
        hidden, cotan, (((0,), (0,)), ((), ())), preferred_element_type=jnp.float32
    )
    back_split = back_pre.reshape(back_pre.shape[0], picked.shape[1], BLK)
    grad_first = jnp.einsum(
        "rckb,rcd->ckbd", picked, back_split, preferred_element_type=jnp.float32
    )
    return (grad_first, grad_second)


def add_rounded(first_cot, second_cot):
    return (first_cot.astype(jnp.float32) + second_cot.astype(jnp.float32)).astype(jnp.bfloat16)


def body(lengths, pattern, first_blocks, second_weight, frames, frame_ok):
    seg_rows = frames.shape[0]
    offset = lax.axis_index("traj") * seg_rows
    picked, squash, hidden, codes = encode(frames, pattern, first_blocks, second_weight)
    flags = frame_ok[:LAG].astype(jnp.float32)
    far_codes, far_flags = (
        from_behind(codes[:LAG].astype(jnp.bfloat16), "traj", -1).astype(jnp.float32),
        from_behind(flags.astype(jnp.bfloat16), "traj", -1).astype(flags.dtype),
    )
    codes_b = jnp.concatenate([codes[LAG:], far_codes], axis=0)
    ok_lagged = jnp.concatenate([frame_ok[LAG:].astype(jnp.float32), far_flags], axis=0)
    weights = pair_weights(lengths, frame_ok, ok_lagged, offset)
    local_stats = moments(weights, codes, codes_b)
    stats = lax.psum(
        (
            local_stats[0],
            local_stats[1],
            local_stats[2],
            local_stats[3],
            local_stats[4],
            local_stats[5],
        ),
        "traj",
    )
    score, pull = jax.vjp(vamp_score, *stats)
    grads = pull(jnp.ones_like(score))
    cot_a, cot_b = code_cotangents(weights, codes, codes_b, grads)
    returned = from_behind(cot_b[seg_rows - LAG :], "traj", 1)
    cot_shifted = jnp.concatenate([returned, cot_b[: seg_rows - LAG]], axis=0)
    frame_cot = add_rounded(cot_a, cot_shifted)
    first_t, second_t = role_terms(picked, squash, hidden, frame_cot, second_weight)
    grad_first = first_t.reshape(-1, BLK)
    share_first, share_second = (
        lax.psum_scatter(grad_first, "traj", scatter_dimension=0, tiled=True),
        lax.psum_scatter(second_t, "traj", scatter_dimension=0, tiled=True),
    )
    return (score.reshape(1), share_first, share_second)


def solution(mesh):
    placed = (P("groups"), P(), P(), P(), P(("groups", "traj"), None), P(("groups", "traj")))
    return jax.shard_map(
        body,
        mesh=mesh,
        in_specs=placed,
        out_specs=(P("groups"), P(("groups", "traj"), None), P(("groups", "traj"), None)),
        check_vma=False,
    )
```

profile of v0, /device:TPU:0, one launch (start us, length us, event | category | flops | bytes accessed | tf_op | source)
XLA Modules:
  0.0 862.8 jit_solution(8747319875841455101)
XLA Ops:
  7.2 6.6 copy.89
  13.8 6.4 copy.90
  20.3 7.7 gather_fusion
  28.1 7.7 multiply_subtract_fusion
  43.2 3.1 fusion.7
  46.3 3.1 fusion.5
  49.4 3.1 fusion.3
  53.4 37.3 %all-reduce.1 = (f32[512]{0:T(512)S(1)}, f32[]{:T(128)}, f32[512]{0:T(512)S(1)}) all-reduce(f32[512]{0:T(512)S(1)} %get-tuple-element.130, f32[]{:T(128)} %get-tuple-element.175, f32[512]{0:T(512)S(1)} %get-tuple-element.129), channel_id=1, replica_groups=mesh['groups'=2,'traj'=16] {'traj'}, use_global_device_ids=true, to_apply=%region_18.20 | all-reduce | flops 1025 | bytes 8200 | tf_op jit(solution)/shard_map/psum | solution.py:120
  91.9 69.6 %all-reduce.5.cloned.1.call-done = (f32[512,512]{0,1:T(8,128)}, f32[512,512]{0,1:T(8,128)}, f32[512,512]{0,1:T(8,128)}) async-done(((f32[512,512]{0,1:T(8,128)}, f32[512,512]{0,1:T(8,128)}, f32[512,512]{0,1:T(8,128)}), (f32[512,512]{0,1:T(8,128)}, f32[512,512]{0,1:T(8,128)}, f32[512,512]{0,1:T(8,128)})) %all-reduce.5.cloned.1.call-update) | async-done | bytes 3145744 | tf_op jit(solution)/shard_map/psum | solution.py:120
  161.4 4.1 select_add_fusion.1
  165.5 2.5 copy.96
  170.8 11.7 %cholesky.286 = f32[128,128]{1,0:T(8,128)S(1)} custom-call(f32[128,128]{1,0:T(8,128)S(1)} %cholesky.426), custom_call_target="Cholesky" | custom-call | tf_op jit(solution)/shard_map/jvp(jit(cholesky))/cholesky | solution.py:27
  183.8 9.8 %custom-call.41 = f32[1,128,128]{1,2,0:T(8,128)S(1)} custom-call(f32[1,128,128]{2,1,0:T(8,128)S(1)} %get-tuple-element.200), custom_call_target="InvertDiagBlocksLowerTriangular" | custom-call | tf_op jit(solution)/shard_map/jvp(jit(cholesky))/cholesky | solution.py:27
  196.8 11.7 %cholesky.305 = f32[128,128]{1,0:T(8,128)S(1)} custom-call(f32[128,128]{1,0:T(8,128)S(1)} %cholesky.430), custom_call_target="Cholesky" | custom-call | tf_op jit(solution)/shard_map/jvp(jit(cholesky))/cholesky | solution.py:27
  210.4 10.2 %custom-call.42 = f32[1,128,128]{1,2,0:T(8,128)S(1)} custom-call(f32[1,128,128]{2,1,0:T(8,128)S(1)} %get-tuple-element.197), custom_call_target="InvertDiagBlocksLowerTriangular" | custom-call | tf_op jit(solution)/shard_map/jvp(jit(cholesky))/cholesky | solution.py:27
  223.1 11.7 %cholesky.326 = f32[128,128]{1,0:T(8,128)S(1)} custom-call(f32[128,128]{1,0:T(8,128)S(1)} %cholesky.435), custom_call_target="Cholesky" | custom-call | tf_op jit(solution)/shard_map/jvp(jit(cholesky))/cholesky | solution.py:27
  236.1 9.8 %custom-call.43 = f32[1,128,128]{1,2,0:T(8,128)S(1)} custom-call(f32[1,128,128]{2,1,0:T(8,128)S(1)} %get-tuple-element.194), custom_call_target="InvertDiagBlocksLowerTriangular" | custom-call | tf_op jit(solution)/shard_map/jvp(jit(cholesky))/cholesky | solution.py:27
  248.2 11.9 %cholesky.343 = f32[128,128]{1,0:T(8,128)S(1)} custom-call(f32[128,128]{1,0:T(8,128)S(1)} %convolution_subtract_fusion.35), custom_call_target="Cholesky" | custom-call | tf_op jit(solution)/shard_map/jvp(jit(cholesky))/cholesky | solution.py:27
  264.0 2.9 fusion.46
  266.9 11.5 %while.23 = (s32[]{:T(128)}, f32[512,512]{1,0:T(8,128)}, s32[4,2]{0,1:T(2,128)S(1)}, f32[4,128,128]{2,1,0:T(8,128)S(1)}, s32[]{:T(128)}) while((s32[]{:T(128)}, f32[512,512]{1,0:T(8,128)}, s32[4,2]{0,1:T(2,128)S(1)}, f32[4,128,128]{2,1,0:T(8,128)S(1)}, s32[]{:T(128)}) %tuple.142), condition=%wide.while_cond.clone, body=%wide.while_body.clone.sunk | while | flops 2 | bytes 131181 | solution.py:29
  267.6 2.3 bitcast_dynamic-update-slice_fusion.9
  270.5 2.3 bitcast_dynamic-update-slice_fusion.9
  279.2 40.1 %custom-call.48 = f32[4,128,128]{1,2,0:T(8,128)S(1)} custom-call(f32[4,128,128]{2,1,0:T(8,128)} %copy-done.33), custom_call_target="InvertDiagBlocksLowerTriangular" | custom-call | tf_op jit(solution)/shard_map/jvp(jit(_solve_triangular))/triangular_solve | solution.py:29
  323.1 11.7 %cholesky.358 = f32[128,128]{1,0:T(8,128)S(1)} custom-call(f32[128,128]{1,0:T(8,128)S(1)} %cholesky.439), custom_call_target="Cholesky" | custom-call | tf_op jit(solution)/shard_map/jvp(jit(cholesky))/cholesky | solution.py:26
  335.5 9.8 %custom-call.44 = f32[1,128,128]{1,2,0:T(8,128)S(1)} custom-call(f32[1,128,128]{2,1,0:T(8,128)S(1)} %get-tuple-element.210), custom_call_target="InvertDiagBlocksLowerTriangular" | custom-call | tf_op jit(solution)/shard_map/jvp(jit(cholesky))/cholesky | solution.py:26
  348.5 11.7 %cholesky.377 = f32[128,128]{1,0:T(8,128)S(1)} custom-call(f32[128,128]{1,0:T(8,128)S(1)} %cholesky.443), custom_call_target="Cholesky" | custom-call | tf_op jit(solution)/shard_map/jvp(jit(cholesky))/cholesky | solution.py:26
  362.2 10.2 %custom-call.45 = f32[1,128,128]{1,2,0:T(8,128)S(1)} custom-call(f32[1,128,128]{2,1,0:T(8,128)S(1)} %get-tuple-element.207), custom_call_target="InvertDiagBlocksLowerTriangular" | custom-call | tf_op jit(solution)/shard_map/jvp(jit(cholesky))/cholesky | solution.py:26
  375.5 13.2 %cholesky.398 = f32[128,128]{1,0:T(8,128)} custom-call(f32[128,128]{1,0:T(8,128)} %cholesky.448), custom_call_target="Cholesky" | custom-call | tf_op jit(solution)/shard_map/jvp(jit(cholesky))/cholesky | solution.py:26
  390.7 11.3 %custom-call.46 = f32[1,128,128]{1,2,0:T(8,128)} custom-call(f32[1,128,128]{2,1,0:T(8,128)} %get-tuple-element.204), custom_call_target="InvertDiagBlocksLowerTriangular" | custom-call | tf_op jit(solution)/shard_map/jvp(jit(cholesky))/cholesky | solution.py:26
  404.3 11.7 %cholesky.415 = f32[128,128]{1,0:T(8,128)S(1)} custom-call(f32[128,128]{1,0:T(8,128)S(1)} %convolution_subtract_fusion.34), custom_call_target="Cholesky" | custom-call | tf_op jit(solution)/shard_map/jvp(jit(cholesky))/cholesky | solution.py:26
  421.6 14.2 %while.22 = (s32[]{:T(128)}, f32[512,512]{1,0:T(8,128)}, s32[4,2]{0,1:T(2,128)S(1)}, f32[4,128,128]{2,1,0:T(8,128)}, s32[]{:T(128)}) while((s32[]{:T(128)}, f32[512,512]{1,0:T(8,128)}, s32[4,2]{0,1:T(2,128)S(1)}, f32[4,128,128]{2,1,0:T(8,128)}, s32[]{:T(128)}) %tuple.158), condition=%wide.while_cond, body=%wide.while_body.sunk | while | flops 2 | bytes 132705 | solution.py:28
  422.2 2.9 bitcast_dynamic-update-slice_fusion.8
  425.8 2.9 bitcast_dynamic-update-slice_fusion.8
  429.4 2.9 bitcast_dynamic-update-slice_fusion.8
  432.9 2.8 bitcast_dynamic-update-slice_fusion.8
  435.8 40.7 %custom-call.47 = f32[4,128,128]{1,2,0:T(8,128)} custom-call(f32[4,128,128]{2,1,0:T(8,128)} %get-tuple-element.109), custom_call_target="InvertDiagBlocksLowerTriangular" | custom-call | tf_op jit(solution)/shard_map/jvp(jit(_solve_triangular))/triangular_solve | solution.py:28
  484.2 2.5 convolution_subtract_fusion.29
  493.0 2.9 fusion.142
  499.3 4.5 fusion.99
  509.2 3.1 convolution_subtract_fusion.26
  526.4 2.8 fusion.15
  529.3 11.2 %while.24 = (s32[]{:T(128)}, f32[512,512]{1,0:T(8,128)}, s32[4,2]{0,1:T(2,128)S(1)}, f32[4,128,128]{2,1,0:T(8,128)S(1)}, s32[]{:T(128)}) while((s32[]{:T(128)}, f32[512,512]{1,0:T(8,128)}, s32[4,2]{0,1:T(2,128)S(1)}, f32[4,128,128]{2,1,0:T(8,128)S(1)}, s32[]{:T(128)}) %tuple.159), condition=%wide.while_cond.1, body=%wide.while_body.1.sunk | while | flops 2 | bytes 131181 | solution.py:26
  540.5 39.5 %custom-call.52 = f32[4,128,128]{1,2,0:T(8,128)S(1)} custom-call(f32[4,128,128]{2,1,0:T(8,128)S(1)} %get-tuple-element.114), custom_call_target="InvertDiagBlocksLowerTriangular" | custom-call | tf_op jit(solution)/shard_map/transpose(jvp(jit(cholesky)))/triangular_solve/custom-call.0 | solution.py:26
  591.8 2.5 convolution_subtract_fusion.23
  596.5 2.6 copy.114
  608.8 2.9 fusion.12
  611.7 11.5 %while.25 = (s32[]{:T(128)}, f32[512,512]{1,0:T(8,128)}, s32[4,2]{0,1:T(2,128)S(1)}, f32[4,128,128]{2,1,0:T(8,128)S(1)}, s32[]{:T(128)}) while((s32[]{:T(128)}, f32[512,512]{1,0:T(8,128)}, s32[4,2]{0,1:T(2,128)S(1)}, f32[4,128,128]{2,1,0:T(8,128)S(1)}, s32[]{:T(128)}) %tuple.160), condition=%wide.while_cond.1.clone.4, body=%wide.while_body.1.clone.4.sunk | while | flops 2 | bytes 131181 | solution.py:27
  612.3 2.3 bitcast_dynamic-update-slice_fusion.11
  615.2 2.3 bitcast_dynamic-update-slice_fusion.11
  618.1 2.3 bitcast_dynamic-update-slice_fusion.11
  623.2 39.5 %custom-call.55 = f32[4,128,128]{1,2,0:T(8,128)S(1)} custom-call(f32[4,128,128]{2,1,0:T(8,128)S(1)} %get-tuple-element.117), custom_call_target="InvertDiagBlocksLowerTriangular" | custom-call | tf_op jit(solution)/shard_map/transpose(jvp(jit(cholesky)))/triangular_solve/custom-call.0 | solution.py:27
  674.7 2.5 convolution_subtract_fusion.20
  679.7 3.4 fusion.36
  683.1 2.7 copy.115
  688.6 4.4 fusion.141
  693.1 2.8 multiply_reduce_fusion.4
  695.8 2.6 copy.120
  699.0 4.0 fusion.17
  707.8 3.1 convolution_add_fusion.2
  710.9 3.5 fusion.21
  718.5 11.5 %copy.91 = bf16[8,8,512,128]{2,3,1,0:T(8,128)(2,1)} copy(bf16[8,8,512,128]{3,2,1,0:T(8,128)(2,1)} %bitcast.331) | data formatting | bytes 16777216 | tf_op jit(solution)/shard_map/gather | solution.py:44
  732.3 8.0 fusion
  740.9 37.0 %reduce-scatter.5.cloned.1.call-done = f32[64,512]{1,0:T(8,128)} async-done(((f32[1024,512]{1,0:T(8,128)}), f32[64,512]{1,0:T(8,128)}) %reduce-scatter.5.cloned.1.call-update) | async-done | bytes 131088 | tf_op jit(solution)/shard_map/reduce_scatter | solution.py:141
  777.9 76.8 %reduce-scatter.3.cloned.1.call-done = f32[512,128]{1,0:T(8,128)} async-done(((f32[8192,128]{1,0:T(8,128)}), f32[512,128]{1,0:T(8,128)}) %reduce-scatter.3.cloned.1.call-update) | async-done | bytes 262160 | tf_op jit(solution)/shard_map/reduce_scatter | solution.py:140
  (279 shorter events, 160.8 us)
Async XLA Ops:
  7.2 20.9 %copy-start = (bf16[8192,128]{1,0:T(8,128)(2,1)S(1)}, bf16[8192,128]{1,0:T(8,128)(2,1)}, u32[]{:S(2)}) copy-start(bf16[8192,128]{1,0:T(8,128)(2,1)} %param.20) | copy-start | bytes 6291460
  7.2 154.3 %all-reduce.5.cloned.1.call-start = ((), (), s32[]{:S(2)}) async-start(), calls=%async_computation.4 | async-start | bytes 6291456 | tf_op jit(solution)/shard_map/psum | solution.py:120
  13.8 6.4 copy-start.36
  28.1 8.7 %copy-start.31 = (bf16[1024,512]{1,0:T(8,128)(2,1)S(1)}, bf16[1024,512]{1,0:T(8,128)(2,1)}, u32[]{:S(2)}) copy-start(bf16[1024,512]{1,0:T(8,128)(2,1)} %param.21) | copy-start | bytes 3145732
  35.8 1.0 copy-start.22
  35.8 3.0 copy-start.35
  35.8 4.4 copy-start.37
  37.5 8.7 %collective-permute-start = (bf16[64,512]{1,0:T(8,128)(2,1)S(1)}, bf16[64,512]{1,0:T(8,128)(2,1)S(1)}, u32[]{:S(2)}, u32[]{:S(2)}) collective-permute-start(bf16[64,512]{1,0:T(8,128)(2,1)S(1)} %slice.505), channel_id=1, source_target_pairs={{1,0},{2,1},{3,2},{4,3},{5,4},{6,5},{7,6},{8,7},{9,8},{10,9},{11,1... | collective-permute-start | bytes 196616 | tf_op jit(solution)/shard_map/ppermute | solution.py:16
  38.9 3.6 collective-permute-start.1
  52.5 725.4 %reduce-scatter.5.cloned.1.call-start = ((), (), s32[]{:S(2)}) async-start(), calls=%async_computation.3 | async-start | bytes 2228224 | tf_op jit(solution)/shard_map/reduce_scatter | solution.py:141
  169.9 1.0 copy-start.14
  278.5 0.7 copy-start.33
  319.3 179.6 %copy-start.16 = (f32[4,128,128]{1,2,0:T(8,128)}, f32[4,128,128]{1,2,0:T(8,128)S(1)}, u32[]{:S(2)}) copy-start(f32[4,128,128]{1,2,0:T(8,128)S(1)} %custom-call.48) | copy-start | bytes 786436
  322.1 1.0 copy-start.15
  347.8 0.7 copy-start.32
  476.5 10.2 %copy-start.17 = (f32[4,128,128]{1,2,0:T(8,128)S(1)}, f32[4,128,128]{1,2,0:T(8,128)}, u32[]{:S(2)}) copy-start(f32[4,128,128]{1,2,0:T(8,128)} %custom-call.47) | copy-start | bytes 786436
  476.5 11.2 %copy-start.8 = (f32[512,512]{1,0:T(8,128)S(1)}, f32[512,512]{1,0:T(8,128)}, u32[]{:S(2)}) copy-start(f32[512,512]{1,0:T(8,128)} %get-tuple-element.410) | copy-start | bytes 3145732
  506.1 2.4 copy-start.11
  508.5 0.7 copy-start.18
  589.4 5.3 copy-start.6
  591.8 2.9 copy-start.12
  594.7 0.7 copy-start.19
  596.5 12.3 %copy-start.5 = (f32[512,512]{1,0:T(8,128)S(1)}, f32[512,512]{1,0:T(8,128)}, u32[]{:S(2)}) copy-start(f32[512,512]{1,0:T(8,128)} %get-tuple-element.192) | copy-start | bytes 3145732
  670.3 7.3 copy-start.4
  671.8 7.9 copy-start.34
  672.2 5.4 copy-start.7
  674.6 3.0 copy-start.13
  677.6 0.7 copy-start.20
  683.1 5.5 copy-start.24
  687.0 6.0 copy-start.2
  687.0 6.0 copy-start.9
  687.0 6.0 copy-start.10
  687.0 6.0 copy-start.25
  687.0 6.0 copy-start.27
  688.6 7.2 copy-start.29
  695.8 10.0 %copy-start.3 = (f32[512,512]{0,1:T(8,128)S(1)}, f32[512,512]{0,1:T(8,128)}, u32[]{:S(2)}) copy-start(f32[512,512]{0,1:T(8,128)} %get-tuple-element.186) | copy-start | bytes 3145732
  703.1 0.8 copy-start.21
  703.9 7.0 collective-permute-start.2
  707.1 3.8 slice-start
  707.1 3.8 copy-start.26
  707.1 3.8 copy-start.28
  707.1 3.8 copy-start.30
  710.9 3.5 copy-start.23
  716.5 138.2 %reduce-scatter.3.cloned.1.call-start = ((), (), s32[]{:S(2)}) async-start(), calls=%async_computation.2 | async-start | bytes 4456448 | tf_op jit(solution)/shard_map/reduce_scatter | solution.py:140
  732.3 122.5 %copy-start.1 = (bf16[8192,128]{1,0:T(8,128)(2,1)S(1)}, bf16[8192,128]{1,0:T(8,128)(2,1)}, u32[]{:S(2)}) copy-start(bf16[8192,128]{1,0:T(8,128)(2,1)} %param.20) | copy-start | bytes 6291460
Sparse Core Ops, SparseCore 0:
  52.6 108.7 all-reduce.4
  716.6 61.2 reduce-scatter.4
  782.9 71.8 reduce-scatter.2
where the time goes:
time: 874 us; the launch traced here: 863 us
  other arithmetic  351 us (40%)
  waiting for transfers between devices  185 us (21%)
  matrix products  149 us (17%)
  local copies, waits for them, and re-layouts  113 us (13%)
  blocking collectives  37.3 us (4%)
  between operations  22.2 us (3%)
    another operation x18, other arithmetic, vamp_score(): factor_a = jnp.linalg.cholesky(cov_aa)  126 us
    another operation x18, other arithmetic, vamp_score(): factor_b = jnp.linalg.cholesky(cov_bb)  121 us
    reduce_scatter x1, waiting for transfers between devices, body(): lax.psum_scatter(grad_first, 'traj', scatter_dimension=0, tiled=True)  76.8 us
    psum x1, waiting for transfers between devices, body(): lax.psum((local_stats[0], local_stats[1], local_stats[2], local_stats[3],...  69.6 us
    another operation x3, other arithmetic, vamp_score(): jax.scipy.linalg.solve_triangular(factor_b, partial_solve.T, lower=True)  43 us
    another operation x2, other arithmetic, vamp_score(): jax.scipy.linalg.solve_triangular(factor_a, cov_ab, lower=True)  42.5 us
    psum x1, blocking collectives, body(): lax.psum((local_stats[0], local_stats[1], local_stats[2], local_stats[3],...  37.3 us
    reduce_scatter x1, waiting for transfers between devices, body(): lax.psum_scatter(second_t, 'traj', scatter_dimension=0, tiled=True)  37 us
  transfers between devices with their start and end apart: 6, of which 4 were waited for; matrix products, arithmetic and copies ran while one was open for 4% of the time, Pallas kernels for 0%

commit v1 on v0

v1 whole, which is shorter than its diff:
```python
import functools

import jax
import jax.numpy as jnp
from jax import lax
from jax.experimental import pallas as pl
from jax.experimental.pallas import tpu as pltpu
from jax.sharding import PartitionSpec as P

BLK = 128
LAG = 64
EPS = 0.01
HIGHEST = lax.Precision.HIGHEST
VMEM = pl.BlockSpec(memory_space=pltpu.VMEM)
SMEM = pl.BlockSpec(memory_space=pltpu.SMEM)
LIMIT = 50 * 1024 * 1024


def from_behind(block, axis, distance):
    devices = range(lax.axis_size(axis))
    route = [(i - distance, i) for i in devices if i - distance in devices]
    return lax.ppermute(block, axis, route)


def pair_weights(lengths, ok_now, ok_lagged, offset):
    positions = offset + jnp.arange(ok_now.shape[0], dtype=jnp.int32)
    bounds = jnp.cumsum(lengths)
    owner_now = jnp.sum((bounds[None, :] <= positions[:, None]).astype(jnp.int32), axis=1)
    owner_lag = jnp.sum((bounds[None, :] <= (positions + LAG)[:, None]).astype(jnp.int32), axis=1)
    keep = (owner_now == owner_lag) & (ok_now > 0.5) & (ok_lagged > 0.5)
    return keep.astype(jnp.float32)


def mm(a, b, dims=((1,), (0,)), precision=HIGHEST):
    return lax.dot_general(
        a, b, (dims, ((), ())), precision=precision, preferred_element_type=jnp.float32
    )


def mm_bf16(a, b, dims=((1,), (0,))):
    return lax.dot_general(a, b, (dims, ((), ())), preferred_element_type=jnp.float32)


def split(x):
    high = x.astype(jnp.bfloat16)
    return high, (x - high.astype(jnp.float32)).astype(jnp.bfloat16)


def mm3(a, b, dims=((1,), (0,))):
    return mm_bf16(a[0], b[0], dims) + (mm_bf16(a[0], b[1], dims) + mm_bf16(a[1], b[0], dims))


def picked_columns(pattern_ref, frames_ref, col, slots):
    parts = []
    for slot in range(slots):
        start = pl.multiple_of(pattern_ref[col, slot] * BLK, BLK)
        parts.append(frames_ref[:, pl.ds(start, BLK)])
    return jnp.concatenate(parts, axis=1)


def encode_kernel(pattern_ref, frames_ref, first_ref, second_ref, squash_ref, hidden_ref, codes_ref):
    cols, slots = pattern_ref.shape
    depth = slots * BLK

    def column(col, _):
        picked = picked_columns(pattern_ref, frames_ref, col, slots)
        blocks = first_ref[pl.ds(pl.multiple_of(col * depth, depth), depth), :]
        squash = jnp.tanh(mm_bf16(picked, blocks))
        at = pl.ds(pl.multiple_of(col * BLK, BLK), BLK)
        squash_ref[:, at] = squash
        hidden_ref[:, at] = squash.astype(jnp.bfloat16)
        return 0

    lax.fori_loop(0, cols, column, 0)
    codes_ref[...] = mm_bf16(hidden_ref[...], second_ref[...])


def moments_kernel(codes_ref, far_ref, weights_ref, out_ref):
    codes = codes_ref[...]
    lagged = jnp.concatenate([codes[LAG:], far_ref[...].astype(jnp.float32)], axis=0)
    weights = weights_ref[...]
    scaled_a = codes * weights
    scaled_b = lagged * weights
    out = codes.shape[1]
    nb = out // BLK
    over_rows = ((0,), (0,))
    at = 0
    for left, right, whole in ((scaled_a, codes, False), (scaled_b, lagged, False), (scaled_a, lagged, True)):
        product = mm(left, right, over_rows)
        for i in range(nb):
            for j in range(0 if whole else i, nb):
                out_ref[pl.ds(at, BLK), :] = product[i * BLK : (i + 1) * BLK, j * BLK : (j + 1) * BLK]
                at += BLK
    sum_a = jnp.sum(scaled_a, axis=0, keepdims=True)
    sum_b = jnp.sum(scaled_b, axis=0, keepdims=True)
    for i in range(nb):
        out_ref[at + i : at + i + 1, :] = sum_a[:, i * BLK : (i + 1) * BLK]
        out_ref[at + nb + i : at + nb + i + 1, :] = sum_b[:, i * BLK : (i + 1) * BLK]
    total = jnp.sum(jnp.broadcast_to(weights, (weights.shape[0], BLK)), axis=0, keepdims=True)
    out_ref[at + 2 * nb : at + 2 * nb + 8, :] = jnp.broadcast_to(total, (8, BLK))


def invert_pair(one, two):
    size = one.shape[0]
    lane = lax.broadcasted_iota(jnp.int32, (size, size), 1)
    sub = lax.broadcasted_iota(jnp.int32, (size, size), 0)
    lane_row = lax.broadcasted_iota(jnp.int32, (1, size), 1)

    def step(m, k):
        column = m[:, k : k + 1]
        row = m[k : k + 1, :]
        inverse = 1.0 / m[k : k + 1, k : k + 1]
        row = jnp.where(lane_row == k, inverse, row * inverse)
        updated = jnp.where(lane == k, 0.0, m) - column * row
        return jnp.where(sub == k, row, updated)

    for k in range(size):
        one, two = step(one, k), step(two, k)
    return one, two


def solve_kernel(stats_ref, codes_ref, far_ref, weights_ref, score_ref, cot_a_ref, cot_b_ref, inv_ref, cross_ref):
    out = codes_ref.shape[1]
    nb = out // BLK
    tri = nb * (nb + 1) // 2
    base = (2 * tri + nb * nb) * BLK
    weight_sum = stats_ref[base + 2 * nb : base + 2 * nb + 1, 0:1]
    scale = 1.0 / weight_sum
    means_a = [stats_ref[base + i : base + i + 1, :] / weight_sum for i in range(nb)]
    means_b = [stats_ref[base + nb + i : base + nb + i + 1, :] / weight_sum for i in range(nb)]
    mean_a = jnp.concatenate(means_a, axis=1)
    mean_b = jnp.concatenate(means_b, axis=1)
    square = lax.broadcasted_iota(jnp.int32, (BLK, BLK), 0) == lax.broadcasted_iota(jnp.int32, (BLK, BLK), 1)
    ridge = jnp.where(square, EPS, 0.0)
    tall_a = [jnp.transpose(jnp.broadcast_to(m, (BLK, BLK))) for m in means_a]
    tall_b = [jnp.transpose(jnp.broadcast_to(m, (BLK, BLK))) for m in means_b]
    at = 0
    for which, tall, flat in ((0, tall_a, means_a), (1, tall_b, means_b)):
        for i in range(nb):
            for j in range(i, nb):
                block = stats_ref[pl.ds(at, BLK), :] / weight_sum - tall[i] * flat[j]
                if i == j:
                    block = block + ridge
                else:
                    inv_ref[which, j * BLK : (j + 1) * BLK, i * BLK : (i + 1) * BLK] = jnp.transpose(block)
                inv_ref[which, i * BLK : (i + 1) * BLK, j * BLK : (j + 1) * BLK] = block
                at += BLK
    for i in range(nb):
        for j in range(nb):
            cross_ref[i * BLK : (i + 1) * BLK, j * BLK : (j + 1) * BLK] = (
                stats_ref[pl.ds(at, BLK), :] / weight_sum - tall_a[i] * means_b[j]
            )
            at += BLK

    def pivot(block, _):
        here = pl.ds(pl.multiple_of(block * BLK, BLK), BLK)
        inverses = invert_pair(inv_ref[0, here, here], inv_ref[1, here, here])
        for which in range(2):
            panel = inv_ref[which, :, here]
            inv_ref[which, :, here] = jnp.zeros_like(panel)
            inv_ref[which, here, here] = jnp.zeros((BLK, BLK), jnp.float32)
            rows = mm(inverses[which], inv_ref[which, here, :])
            inv_ref[which, here, :] = rows
            inv_ref[which, here, here] = inverses[which]
            rows = inv_ref[which, here, :]
            inv_ref[which] = inv_ref[which] - mm(panel, rows)
            inv_ref[which, here, :] = rows
        return 0

    lax.fori_loop(0, nb, pivot, 0)
    inv_a, inv_b, cross = split(inv_ref[0]), split(inv_ref[1]), split(cross_ref[...])
    pull_a = mm3(inv_a, cross)
    pull_b = mm3(inv_b, cross, ((1,), (1,)))
    pull_a_parts = split(pull_a)
    middle = mm3(pull_a_parts, inv_b)
    score_ref[...] = jnp.sum(middle * cross_ref[...], axis=0, keepdims=True) / out
    middle = split(middle)
    codes = codes_ref[...]
    lagged = jnp.concatenate([codes[LAG:], far_ref[...].astype(jnp.float32)], axis=0)
    codes = codes - mean_a
    lagged = lagged - mean_b
    factor = weights_ref[...] * (2.0 / out * scale)
    rest_b = split(lagged - mm3(split(codes), pull_a_parts))
    cot_a_ref[...] = (factor * mm3(rest_b, middle, ((1,), (1,)))).astype(jnp.bfloat16)
    rest_a = split(codes - mm3(split(lagged), split(pull_b)))
    cot_b_ref[...] = (factor * mm3(rest_a, middle)).astype(jnp.bfloat16)


def backward_kernel(
    pattern_ref, frames_ref, second_ref, squash_ref, hidden_ref, cot_a_ref, cot_b_ref, back_ref, first_ref, grad_ref, pre_ref
):
    cols, slots = pattern_ref.shape
    depth = slots * BLK
    rows = cot_b_ref.shape[0]
    shifted = jnp.concatenate([back_ref[...], cot_b_ref[: rows - LAG, :]], axis=0)
    cotan = (cot_a_ref[...].astype(jnp.float32) + shifted.astype(jnp.float32)).astype(jnp.bfloat16)
    grad_ref[...] = mm_bf16(hidden_ref[...], cotan, ((0,), (0,)))
    squash = squash_ref[...]
    pre_ref[...] = (mm_bf16(cotan, second_ref[...], ((1,), (1,))) * (1.0 - squash * squash)).astype(jnp.bfloat16)

    def column(col, _):
        picked = picked_columns(pattern_ref, frames_ref, col, slots)
        back = pre_ref[:, pl.ds(pl.multiple_of(col * BLK, BLK), BLK)]
        first_ref[pl.ds(pl.multiple_of(col * depth, depth), depth), :] = mm_bf16(picked, back, ((0,), (0,)))
        return 0

    lax.fori_loop(0, cols, column, 0)


def call(kernel, shapes, specs, scratch=()):
    return pl.pallas_call(
        kernel,
        out_shape=[jax.ShapeDtypeStruct(s, d) for s, d in shapes],
        in_specs=specs,
        out_specs=[VMEM] * len(shapes),
        scratch_shapes=list(scratch),
        compiler_params=pltpu.CompilerParams(vmem_limit_bytes=LIMIT),
    )


def body(lengths, pattern, first_blocks, second_weight, frames, frame_ok):
    f32, bf16 = jnp.float32, jnp.bfloat16
    rows = frames.shape[0]
    hid, out = second_weight.shape
    nb = out // BLK
    offset = lax.axis_index("traj") * rows
    squash, hidden, codes = call(
        encode_kernel, [((rows, hid), f32), ((rows, hid), bf16), ((rows, out), f32)], [SMEM, VMEM, VMEM, VMEM]
    )(pattern, frames, first_blocks, second_weight)
    far_flags = from_behind(frame_ok[:LAG].astype(bf16), "traj", -1).astype(f32)
    far_codes = from_behind(codes[:LAG].astype(bf16), "traj", -1)
    ok_lagged = jnp.concatenate([frame_ok[LAG:].astype(f32), far_flags], axis=0)
    weights = pair_weights(lengths, frame_ok, ok_lagged, offset)[:, None]
    stat_rows = (nb * (nb + 1) + nb * nb) * BLK + 2 * nb + 8
    (local_stats,) = call(moments_kernel, [((stat_rows, BLK), f32)], [VMEM] * 3)(codes, far_codes, weights)
    stats = lax.psum(local_stats, "traj")
    score, cot_a, cot_b = call(
        solve_kernel,
        [((1, out), f32), ((rows, out), bf16), ((rows, out), bf16)],
        [VMEM] * 4,
        [pltpu.VMEM((2, out, out), f32), pltpu.VMEM((out, out), f32)],
    )(stats, codes, far_codes, weights)
    returned = from_behind(cot_b[rows - LAG :], "traj", 1)
    grad_first, grad_second = call(
        backward_kernel,
        [(first_blocks.shape, f32), ((hid, out), f32)],
        [SMEM] + [VMEM] * 7,
        [pltpu.VMEM((rows, hid), bf16)],
    )(pattern, frames, second_weight, squash, hidden, cot_a, cot_b, returned)
    share_first = lax.psum_scatter(grad_first, "traj", scatter_dimension=0, tiled=True)
    share_second = lax.psum_scatter(grad_second, "traj", scatter_dimension=0, tiled=True)
    return (jnp.sum(score).reshape(1), share_first, share_second)


def solution(mesh):
    placed = (P("groups"), P(), P(), P(), P(("groups", "traj"), None), P(("groups", "traj")))
    return jax.shard_map(
        body,
        mesh=mesh,
        in_specs=placed,
        out_specs=(P("groups"), P(("groups", "traj"), None), P(("groups", "traj"), None)),
        check_vma=False,
    )
```

time: 874 us -> 373 us (0.43); the launches traced: 863 us -> 373 us
  other arithmetic: 351 us -> 1.72 us
  matrix products: 149 us -> 0 us
  local copies, waits for them, and re-layouts: 113 us -> 2.1 us
  Pallas kernels: 0 us -> 103 us
  waiting for transfers between devices: 185 us -> 248 us
  blocking collectives: 37.3 us -> 0 us
    another operation x42 -> x2, other arithmetic: 332 us -> 0.86 us  [the longest x18 126 us: vamp_score(): factor_a = jnp.linalg.cholesky(cov_aa)]
    pallas_call x0 -> x4, Pallas kernels: none -> 103 us  [the longest x1 77.7 us: body(): call(solve_kernel, [((1, out), f32), ((rows, out), bf16), ((rows, out), b...]
    another operation x82 -> x0, matrix products: 91.2 us -> none  [the longest x21 29.3 us: vamp_score(): jax.scipy.linalg.solve_triangular(factor_a, cov_ab, lower=True)]
    another operation x66 -> x0, local copies, waits for them, and re-layouts: 59.3 us -> none  [the longest x15 18.6 us: vamp_score(): jax.scipy.linalg.solve_triangular(factor_a, cov_ab, lower=True)]
    dot_general x16 -> x0, matrix products: 57.9 us -> none  [the longest x1 7.97 us: role_terms(): jnp.einsum('rckb,rcd->ckbd', picked, back_split, preferred_element_type=j...]
    psum x1 -> x0, blocking collectives: 37.3 us -> none  [body(): lax.psum((local_stats[0], local_stats[1], local_stats[2], local_stats[3],...]
    psum x1, waiting for transfers between devices: 69.6 us -> 104 us  [body(): stats = lax.psum(local_stats, 'traj')]
    reduce_scatter x1, waiting for transfers between devices: 37 us -> 64 us  [body(): lax.psum_scatter(grad_second, 'traj', scatter_dimension=0, tiled=True)]
  transfers between devices with their start and end apart: 6 -> 6, of which waited for: 4 -> 5; matrix products, arithmetic and copies ran while one was open for 4% -> 0% of each run, Pallas kernels for 0% -> 2%
where the time goes in v1:
time: 373 us
  waiting for transfers between devices  248 us (66%)
  Pallas kernels  103 us (28%)
  between operations  13.9 us (4%)
  starting transfers between devices  4.17 us (1%)
    psum x1, waiting for transfers between devices, body(): stats = lax.psum(local_stats, 'traj')  104 us
    pallas_call x1, Pallas kernels, body(): call(solve_kernel, [((1, out), f32), ((rows, out), bf16), ((rows, out), b...  77.7 us
    reduce_scatter x1, waiting for transfers between devices, body(): lax.psum_scatter(grad_first, 'traj', scatter_dimension=0, tiled=True)  76.1 us
    reduce_scatter x1, waiting for transfers between devices, body(): lax.psum_scatter(grad_second, 'traj', scatter_dimension=0, tiled=True)  64 us
    pallas_call x1, Pallas kernels, body(): call(backward_kernel, [(first_blocks.shape, f32), ((hid, out), f32)], [SM...  10.9 us
    pallas_call x1, Pallas kernels, body(): call(encode_kernel, [((rows, hid), f32), ((rows, hid), bf16), ((rows, out...  7.91 us
  transfers between devices with their start and end apart: 6, of which 5 were waited for; matrix products, arithmetic and copies ran while one was open for 0% of the time, Pallas kernels for 2%

profile of v1, /device:TPU:0, one launch (start us, length us, event | category | flops | bytes accessed | tf_op | source)
XLA Modules:
  0.0 373.0 jit_solution(15982584163820521331)
XLA Ops:
  7.2 0.0 all-reduce.2.cloned.1.call-start
  7.2 0.7 convert.8
  7.9 1.3 collective-permute-start.1
  9.2 0.0 copy-start
  9.2 1.2 copy-done
  10.4 0.0 copy-start.2
  10.4 0.7 copy-done.2
  11.1 0.0 copy-start.4
  11.1 0.0 copy-start.5
  11.1 7.9 %shard_map.85 = (f32[512,1024]{1,0:T(8,128)}, bf16[512,1024]{1,0:T(8,128)(2,1)S(1)}, f32[512,512]{1,0:T(8,128)S(1)}) custom-call(s32[8,8]{1,0:T(8,128)S(1)} %copy-done.2, bf16[512,4096]{1,0:T(8,128)(2,1)} %frames_ref.3, bf16[8192,128]{1,0:T(8,128)(2,1)} %first_ref.1, bf16[1024,512]{1,0:T(8,128)(2,1)S(1)} %copy-done), custom_call_target="tpu_custom_call" | custom-call | tf_op jit(solution)/shard_map/pallas_call | solution.py:227
  19.0 1.3 collective-permute-start
  20.3 0.0 copy-done.4
  20.3 0.1 slice_convert_fusion.1
  20.4 0.0 copy-done.5
  20.4 0.2 reduce-window.8
  20.6 0.1 convert_reduce_fusion
  20.7 0.0 collective-permute-done.1
  20.7 0.1 fusion.2
  20.8 0.1 copy.11.weights_ref
  21.0 1.9 collective-permute-done.far_ref
  22.8 6.7 %shard_map.86 = f32[4624,128]{1,0:T(8,128)} custom-call(f32[512,512]{1,0:T(8,128)S(1)} %get-tuple-element.11.codes_ref, bf16[64,512]{1,0:T(8,128)(2,1)S(1)} %collective-permute-done.far_ref, f32[512,1]{1,0:T(8,128)S(1)} %copy.11.weights_ref), custom_call_target="tpu_custom_call" | custom-call | tf_op jit(solution)/shard_map/pallas_call | solution.py:235
  29.5 0.0 all-reduce.2.cloned.1.call-update
  29.6 0.0 copy-start.1
  29.6 0.0 copy-start.3
  29.6 0.2 reduce-scatter.5.cloned.1.call-start
  29.8 104.3 %all-reduce.2.cloned.1.call-done.stats_ref = f32[4624,128]{1,0:T(8,128)} async-done(((f32[4624,128]{1,0:T(8,128)}), f32[4624,128]{1,0:T(8,128)}) %all-reduce.2.cloned.1.call-update) | async-done | bytes 2367504 | tf_op jit(solution)/shard_map/psum | solution.py:236
  134.1 77.7 %shard_map.87 = (f32[1,512]{1,0:T(1,128)S(1)}, bf16[512,512]{1,0:T(8,128)(2,1)S(1)}, bf16[512,512]{1,0:T(8,128)(2,1)S(1)}) custom-call(f32[4624,128]{1,0:T(8,128)} %all-reduce.2.cloned.1.call-done.stats_ref, f32[512,512]{1,0:T(8,128)S(1)} %get-tuple-element.11.codes_ref, bf16[64,512]{1,0:T(8,128)(2,1)S(1)} %collective-permute-done.far_ref, ...), custom_call_target="tpu_custom_call" | custom-call | tf_op jit(solution)/shard_map/pallas_call | solution.py:237
  211.8 1.3 collective-permute-start.2
  213.1 0.9 collective-permute-done.2.back_ref
  214.0 0.0 copy-done.1
  214.0 0.0 copy-done.3
  214.0 10.9 %shard_map.88 = (f32[8192,128]{1,0:T(8,128)}, f32[1024,512]{1,0:T(8,128)}) custom-call(s32[8,8]{1,0:T(8,128)S(1)} %copy-done.3, bf16[512,4096]{1,0:T(8,128)(2,1)} %frames_ref.3, bf16[1024,512]{1,0:T(8,128)(2,1)S(1)} %copy-done.1, f32[512,1024]{1,0:T(8,128)} %get-tuple-element.13.squash_ref, bf16[512,1024]{1,0:T(8,128)(2,1)S(1)} %get-tuple-element.14.hidden_ref, ...), custom_call_target="tpu_custom_call" | custom-call | tf_op jit(solution)/shard_map/pallas_call | solution.py:244
  224.9 0.0 reduce-scatter.5.cloned.1.call-update
  225.0 0.0 reduce-scatter.3.cloned.1.call-start
  225.0 0.7 reduce-scatter.3.cloned.1.call-update
  225.7 0.6 reduce_sum.29
  226.3 64.0 %reduce-scatter.5.cloned.1.call-done = f32[64,512]{1,0:T(8,128)} async-done(((f32[1024,512]{1,0:T(8,128)}), f32[64,512]{1,0:T(8,128)}) %reduce-scatter.5.cloned.1.call-update) | async-done | bytes 131088 | tf_op jit(solution)/shard_map/reduce_scatter | solution.py:251
  290.3 76.1 %reduce-scatter.3.cloned.1.call-done = f32[512,128]{1,0:T(8,128)} async-done(((f32[8192,128]{1,0:T(8,128)}), f32[512,128]{1,0:T(8,128)}) %reduce-scatter.3.cloned.1.call-update) | async-done | bytes 262160 | tf_op jit(solution)/shard_map/reduce_scatter | solution.py:250
  (5 shorter events, 0.0 us)
Async XLA Ops:
  7.2 126.9 %all-reduce.2.cloned.1.call-start = ((), (), s32[]{:S(2)}) async-start(), calls=%async_computation.2 | async-start | bytes 4734976 | tf_op jit(solution)/shard_map/psum | solution.py:236
  7.9 12.8 %collective-permute-start.1 = (bf16[64]{0:T(256)(128)(2,1)S(1)}, bf16[64]{0:T(256)(128)(2,1)S(1)}, u32[]{:S(2)}, u32[]{:S(2)}) collective-permute-start(bf16[64]{0:T(256)(128)(2,1)S(1)} %slice.16), channel_id=1, source_target_pairs={{1,0},{2,1},{3,2},{4,3},{5,4},{6,5},{7,6},{8,7},{9,8},{10,9},{11,1... | collective-permute-start | bytes 392 | tf_op jit(solution)/shard_map/ppermute | solution.py:22
  9.2 1.2 copy-start
  10.4 0.7 copy-start.2
  11.1 9.2 %copy-start.4 = (s32[512]{0:T(512)S(1)}, s32[512]{0:T(512)}, u32[]{:S(2)}) copy-start(s32[512]{0:T(512)} %param.11) | copy-start | bytes 6148
  11.1 9.3 %copy-start.5 = (s32[4]{0:T(128)S(1)}, s32[4]{0:T(128)}, u32[]{:S(2)}) copy-start(s32[4]{0:T(128)} %param.6) | copy-start | bytes 52
  19.0 3.8 %collective-permute-start = (bf16[64,512]{1,0:T(8,128)(2,1)S(1)}, bf16[64,512]{1,0:T(8,128)(2,1)S(1)}, u32[]{:S(2)}, u32[]{:S(2)}) collective-permute-start(bf16[64,512]{1,0:T(8,128)(2,1)S(1)} %slice.21), channel_id=1, source_target_pairs={{1,0},{2,1},{3,2},{4,3},{5,4},{6,5},{7,6},{8,7},{9,8},{10,9},{11,1... | collective-permute-start | bytes 196616 | tf_op jit(solution)/shard_map/ppermute | solution.py:22
  29.6 184.4 %copy-start.1 = (bf16[1024,512]{1,0:T(8,128)(2,1)S(1)}, bf16[1024,512]{1,0:T(8,128)(2,1)}, u32[]{:S(2)}) copy-start(bf16[1024,512]{1,0:T(8,128)(2,1)} %second_ref.3) | copy-start | bytes 3145732
  29.6 184.4 %copy-start.3 = (s32[8,8]{1,0:T(8,128)S(1)}, s32[8,8]{1,0:T(8,128)}, u32[]{:S(2)}) copy-start(s32[8,8]{1,0:T(8,128)} %pattern_ref.3) | copy-start | bytes 772
  29.6 260.7 %reduce-scatter.5.cloned.1.call-start = ((), (), s32[]{:S(2)}) async-start(), calls=%async_computation.4 | async-start | bytes 2228224 | tf_op jit(solution)/shard_map/reduce_scatter | solution.py:251
  211.8 2.2 collective-permute-start.2
  225.0 141.5 %reduce-scatter.3.cloned.1.call-start = ((), (), s32[]{:S(2)}) async-start(), calls=%async_computation.3 | async-start | bytes 4456448 | tf_op jit(solution)/shard_map/reduce_scatter | solution.py:250
Sparse Core Ops, SparseCore 0:
  29.7 104.3 all-reduce.1
  225.1 65.1 reduce-scatter.4
  294.7 71.6 reduce-scatter.2

commit v2 on v1

--- a/solution.py
+++ b/solution.py
@@ -97,7 +97,8 @@
         out_ref[at + i : at + i + 1, :] = sum_a[:, i * BLK : (i + 1) * BLK]
         out_ref[at + nb + i : at + nb + i + 1, :] = sum_b[:, i * BLK : (i + 1) * BLK]
     total = jnp.sum(jnp.broadcast_to(weights, (weights.shape[0], BLK)), axis=0, keepdims=True)
-    out_ref[at + 2 * nb : at + 2 * nb + 8, :] = jnp.broadcast_to(total, (8, BLK))
+    spare = out_ref.shape[0] - at - 2 * nb
+    out_ref[at + 2 * nb :, :] = jnp.broadcast_to(total, (spare, BLK))
 
 
 def invert_pair(one, two):
@@ -187,24 +188,193 @@
 
 
 def backward_kernel(
-    pattern_ref, frames_ref, second_ref, squash_ref, hidden_ref, cot_a_ref, cot_b_ref, back_ref, first_ref, grad_ref, pre_ref
+    pattern_ref, frames_ref, second_ref, squash_ref, hidden_ref, cot_a_ref, cot_b_ref, back_ref, out_ref, pre_ref
 ):
     cols, slots = pattern_ref.shape
     depth = slots * BLK
     rows = cot_b_ref.shape[0]
     shifted = jnp.concatenate([back_ref[...], cot_b_ref[: rows - LAG, :]], axis=0)
     cotan = (cot_a_ref[...].astype(jnp.float32) + shifted.astype(jnp.float32)).astype(jnp.bfloat16)
-    grad_ref[...] = mm_bf16(hidden_ref[...], cotan, ((0,), (0,)))
+    owners = out_ref.shape[0]
+    top = cols * depth // owners
+    tall = hidden_ref.shape[1] // owners
+    grad = mm_bf16(hidden_ref[...], cotan, ((0,), (0,)))
+    for i in range(grad.shape[1] // BLK):
+        piece = grad[:, i * BLK : (i + 1) * BLK].reshape(owners, tall, BLK)
+        out_ref[:, top + i * tall : top + (i + 1) * tall, :] = piece
     squash = squash_ref[...]
     pre_ref[...] = (mm_bf16(cotan, second_ref[...], ((1,), (1,))) * (1.0 - squash * squash)).astype(jnp.bfloat16)
 
     def column(col, _):
         picked = picked_columns(pattern_ref, frames_ref, col, slots)
         back = pre_ref[:, pl.ds(pl.multiple_of(col * BLK, BLK), BLK)]
-        first_ref[pl.ds(pl.multiple_of(col * depth, depth), depth), :] = mm_bf16(picked, back, ((0,), (0,)))
+        share = mm_bf16(picked, back, ((0,), (0,))).reshape(depth // top, top, BLK)
+        out_ref[pl.ds(col * (depth // top), depth // top), :top, :] = share
         return 0
 
     lax.fori_loop(0, cols, column, 0)
+
+
+def bit_orders(devices):
+    bits = devices.bit_length() - 1
+    turn = 1 + (bits - 1) // 2
+    return list(range(bits)), [0] + list(range(turn, bits)) + list(range(1, turn))
+
+
+def stage_shapes(devices, order):
+    left = list(range(devices.bit_length() - 1))
+    shapes = []
+    for bit in order:
+        place = left.index(bit)
+        shapes.append((2 ** (len(left) - 1 - place), 2**place))
+        left.remove(bit)
+    return shapes
+
+
+class Exchange:
+    def __init__(self, devices, order, lo, rows, wire):
+        self.order, self.shapes = order, stage_shapes(devices, order)
+        self.lo, self.rows, self.wire = lo, rows, wire
+
+    def scratch(self, gather):
+        wide = [(hi, 2, low, self.rows, BLK) for hi, low in self.shapes]
+        half = [(hi, low, self.rows, BLK) for hi, low in self.shapes]
+        count = len(self.order)
+        out = [pltpu.VMEM(s, jnp.float32) for s in wide[1:]]
+        out += [pltpu.VMEM(s, self.wire) for s in half]
+        out += [pltpu.VMEM(s, self.wire) for s in half]
+        if gather:
+            out += [pltpu.VMEM(s, jnp.float32) for s in wide]
+        return out + [pltpu.SemaphoreType.DMA((2 * count,)), pltpu.SemaphoreType.DMA((2 * count,))]
+
+    def bind(self, x_ref, refs, gather, me):
+        count = len(self.order)
+        self.x_ref, self.me = x_ref, me
+        self.acc, refs = [None] + list(refs[: count - 1]), refs[count - 1 :]
+        self.send, refs = refs[:count], refs[count:]
+        self.recv, refs = refs[:count], refs[count:]
+        if gather:
+            self.full, refs = refs[:count], refs[count:]
+        self.send_sem, self.recv_sem = refs
+        self.bits = [(me // 2**b) % 2 for b in self.order]
+        self.partners = [me + (1 - 2 * bit) * 2**b for bit, b in zip(self.bits, self.order)]
+        self.copies = {}
+
+    def part(self, stage, which):
+        if stage == 0:
+            hi, low = self.shapes[0]
+            got = self.x_ref[:, which, self.lo : self.lo + self.rows, :]
+            return got.reshape(hi, low, self.rows, BLK)
+        return self.acc[stage][:, which]
+
+    def copy(self, key, stage, src, dst):
+        copy = pltpu.make_async_remote_copy(
+            src_ref=src,
+            dst_ref=dst,
+            send_sem=self.send_sem.at[key],
+            recv_sem=self.recv_sem.at[key],
+            device_id={"traj": self.partners[stage]},
+            device_id_type=pl.DeviceIdType.MESH,
+        )
+        copy.start()
+        self.copies[key] = copy
+
+    def start(self, stage):
+        self.send[stage][...] = self.part(stage, 1 - self.bits[stage]).astype(self.wire)
+        self.copy(stage, stage, self.send[stage], self.recv[stage])
+
+    def finish(self, stage):
+        self.copies[stage].wait()
+        total = self.part(stage, self.bits[stage]) + self.recv[stage][...].astype(jnp.float32)
+        if stage + 1 < len(self.order):
+            self.acc[stage + 1][...] = total.reshape(self.acc[stage + 1].shape)
+            return None
+        return total
+
+    def start_gather(self, stage, mine):
+        hi, low = self.shapes[stage]
+        bit = self.bits[stage]
+        self.full[stage][:, bit] = mine.reshape(hi, low, self.rows, BLK)
+        place = self.full[stage].at[:, bit]
+        self.copy(len(self.order) + stage, stage, place, place)
+
+    def finish_gather(self, stage):
+        self.copies[len(self.order) + stage].wait()
+        return self.full[stage][...]
+
+
+def greet(partners):
+    barrier = pltpu.get_barrier_semaphore()
+    for partner in partners:
+        pl.semaphore_signal(
+            barrier, inc=1, device_id={"traj": partner}, device_id_type=pl.DeviceIdType.MESH
+        )
+    pl.semaphore_wait(barrier, len(partners))
+
+
+def run_halving(exchanges):
+    stages = len(exchanges[0].order)
+    for stage in range(stages):
+        for ex in exchanges:
+            if stage > 0:
+                ex.finish(stage - 1)
+            ex.start(stage)
+    return [ex.finish(stages - 1) for ex in exchanges]
+
+
+def bind_all(exchanges, x_ref, refs, gather):
+    me = lax.axis_index("traj")
+    for ex in exchanges:
+        count = len(ex.scratch(gather))
+        ex.bind(x_ref, refs[:count], gather, me)
+        refs = refs[count:]
+    greet(exchanges[0].partners)
+
+
+def reduce_kernel(exchanges, x_ref, out_ref, *refs):
+    bind_all(exchanges, x_ref, refs, True)
+    mine = run_halving(exchanges)
+    stages = len(exchanges[0].order)
+    for stage in reversed(range(stages)):
+        for i, ex in enumerate(exchanges):
+            if stage + 1 < stages:
+                mine[i] = ex.finish_gather(stage + 1)
+            ex.start_gather(stage, mine[i])
+    for ex in exchanges:
+        whole = ex.finish_gather(0)
+        out_ref[:, :, ex.lo : ex.lo + ex.rows, :] = whole.reshape(-1, 2, ex.rows, BLK)
+
+
+def scatter_kernel(exchanges, x_ref, first_ref, second_ref, *refs):
+    bind_all(exchanges, x_ref, refs[1:], False)
+    chunk_ref = refs[0]
+    for ex, total in zip(exchanges, run_halving(exchanges)):
+        chunk_ref[ex.lo : ex.lo + ex.rows, :] = total.reshape(ex.rows, BLK)
+    top = first_ref.shape[0]
+    first_ref[...] = chunk_ref[:top, :]
+    tall, wide = second_ref.shape
+    for i in range(wide // BLK):
+        second_ref[:, i * BLK : (i + 1) * BLK] = chunk_ref[top + i * tall : top + (i + 1) * tall, :]
+
+
+def exchanges_for(devices, rows, wire, align):
+    head = -(-(rows // 2) // align) * align
+    one, two = bit_orders(devices)
+    return [Exchange(devices, one, 0, head, wire), Exchange(devices, two, head, rows - head, wire)]
+
+
+def exchange_call(kernel, exchanges, shapes, gather, ident, extra=()):
+    scratch = list(extra) + [s for ex in exchanges for s in ex.scratch(gather)]
+    return pl.pallas_call(
+        functools.partial(kernel, exchanges),
+        out_shape=[jax.ShapeDtypeStruct(s, jnp.float32) for s in shapes],
+        in_specs=[VMEM],
+        out_specs=[VMEM] * len(shapes),
+        scratch_shapes=scratch,
+        compiler_params=pltpu.CompilerParams(
+            collective_id=ident, has_side_effects=True, vmem_limit_bytes=LIMIT
+        ),
+    )
 
 
 def call(kernel, shapes, specs, scratch=()):
@@ -231,9 +401,15 @@
     far_codes = from_behind(codes[:LAG].astype(bf16), "traj", -1)
     ok_lagged = jnp.concatenate([frame_ok[LAG:].astype(f32), far_flags], axis=0)
     weights = pair_weights(lengths, frame_ok, ok_lagged, offset)[:, None]
-    stat_rows = (nb * (nb + 1) + nb * nb) * BLK + 2 * nb + 8
-    (local_stats,) = call(moments_kernel, [((stat_rows, BLK), f32)], [VMEM] * 3)(codes, far_codes, weights)
-    stats = lax.psum(local_stats, "traj")
+    devices = lax.axis_size("traj")
+    used = (nb * (nb + 1) + nb * nb) * BLK + 2 * nb + 8
+    per = -(-used // (8 * devices)) * 8
+    (local_stats,) = call(moments_kernel, [((devices * per, BLK), f32)], [VMEM] * 3)(codes, far_codes, weights)
+    halves = (devices // 2, 2, per, BLK)
+    (stats,) = exchange_call(reduce_kernel, exchanges_for(devices, per, f32, 8), [halves], True, 0)(
+        local_stats.reshape(halves)
+    )
+    stats = stats.reshape(devices * per, BLK)
     score, cot_a, cot_b = call(
         solve_kernel,
         [((1, out), f32), ((rows, out), bf16), ((rows, out), bf16)],
@@ -241,14 +417,19 @@
         [pltpu.VMEM((2, out, out), f32), pltpu.VMEM((out, out), f32)],
     )(stats, codes, far_codes, weights)
     returned = from_behind(cot_b[rows - LAG :], "traj", 1)
-    grad_first, grad_second = call(
-        backward_kernel,
-        [(first_blocks.shape, f32), ((hid, out), f32)],
-        [SMEM] + [VMEM] * 7,
-        [pltpu.VMEM((rows, hid), bf16)],
+    top, tall = first_blocks.shape[0] // devices, hid // devices
+    chunk = top + tall * nb
+    (grads,) = call(
+        backward_kernel, [((devices, chunk, BLK), f32)], [SMEM] + [VMEM] * 7, [pltpu.VMEM((rows, hid), bf16)]
     )(pattern, frames, second_weight, squash, hidden, cot_a, cot_b, returned)
-    share_first = lax.psum_scatter(grad_first, "traj", scatter_dimension=0, tiled=True)
-    share_second = lax.psum_scatter(grad_second, "traj", scatter_dimension=0, tiled=True)
+    share_first, share_second = exchange_call(
+        scatter_kernel,
+        exchanges_for(devices, chunk, bf16, 16),
+        [(top, BLK), (tall, out)],
+        False,
+        1,
+        [pltpu.VMEM((chunk, BLK), f32)],
+    )(grads.reshape(devices // 2, 2, chunk, BLK))
     return (jnp.sum(score).reshape(1), share_first, share_second)
 
 

time: 373 us -> 215 us (0.58)
  waiting for transfers between devices: 248 us -> 2.14 us
  Pallas kernels: 103 us -> 195 us
  between operations: 13.9 us -> 0.77 us
  local copies, waits for them, and re-layouts: 2.1 us -> 9.99 us
    reduce_scatter x2 -> x0, waiting for transfers between devices: 140 us -> none  [the longest x1 76.1 us: body(): lax.psum_scatter(grad_first, 'traj', scatter_dimension=0, tiled=True)]
    psum x1 -> x0, waiting for transfers between devices: 104 us -> none  [body(): stats = lax.psum(local_stats, 'traj')]
    pallas_call x2 -> x4, Pallas kernels: 17.7 us -> 109 us  [the longest x1 54.2 us: body(): exchange_call(reduce_kernel, exchanges_for(devices, per, f32, 8), [halves...]
    unnamed x12 -> x26, local copies, waits for them, and re-layouts: 1.93 us -> 9.83 us
  transfers between devices with their start and end apart: 6 -> 3, of which waited for: 5 -> 2; matrix products, arithmetic and copies ran while one was open for 0% -> 1% of each run, Pallas kernels for 2% -> 4%
where the time goes in v2:
time: 215 us; the launch traced here: 214 us
  Pallas kernels  195 us (91%)
  local copies, waits for them, and re-layouts  9.99 us (5%)
  starting transfers between devices  4.83 us (2%)
    pallas_call x1, Pallas kernels, body(): call(solve_kernel, [((1, out), f32), ((rows, out), bf16), ((rows, out), b...  78 us
    pallas_call x1, Pallas kernels, body(): exchange_call(reduce_kernel, exchanges_for(devices, per, f32, 8), [halves...  54.2 us
    pallas_call x1, Pallas kernels, body(): exchange_call(scatter_kernel, exchanges_for(devices, chunk, bf16, 16), [(...  38.3 us
    pallas_call x1, Pallas kernels, body(): call(backward_kernel, [((devices, chunk, BLK), f32)], [SMEM] + [VMEM] * 7...  11.1 us
    unnamed x26, local copies, waits for them, and re-layouts  9.83 us
    pallas_call x1, Pallas kernels, body(): call(encode_kernel, [((rows, hid), f32), ((rows, hid), bf16), ((rows, out...  7.93 us
    pallas_call x1, Pallas kernels, body(): call(moments_kernel, [((devices * per, BLK), f32)], [VMEM] * 3)  5.25 us
    ppermute x3, starting transfers between devices, from_behind(): return lax.ppermute(block, axis, route)  4.83 us
  transfers between devices with their start and end apart: 3, of which 2 were waited for; matrix products, arithmetic and copies ran while one was open for 1% of the time, Pallas kernels for 4%

profile of v2, /device:TPU:0, one launch (start us, length us, event | category | flops | bytes accessed | tf_op | source)
XLA Modules:
  0.0 214.3 jit_solution(1059258571581873559)
XLA Ops:
  0.6 0.7 convert.8
  1.3 1.3 collective-permute-start.1
  2.6 0.0 copy-start.2
  2.6 1.2 copy-done.2
  3.8 0.0 copy-start.8
  3.8 0.7 copy-done.8
  4.5 0.0 copy-start.10
  4.5 0.0 copy-start.11
  4.5 7.9 %shard_map.85 = (f32[512,1024]{1,0:T(8,128)}, bf16[512,1024]{1,0:T(8,128)(2,1)S(1)}, f32[512,512]{1,0:T(8,128)S(1)}) custom-call(s32[8,8]{1,0:T(8,128)S(1)} %copy-done.8, bf16[512,4096]{1,0:T(8,128)(2,1)} %frames_ref.3, bf16[8192,128]{1,0:T(8,128)(2,1)} %first_ref.1, bf16[1024,512]{1,0:T(8,128)(2,1)S(1)} %copy-done.2), custom_call_target="tpu_custom_call" | custom-call | tf_op jit(solution)/shard_map/pallas_call | solution.py:397
  12.5 1.3 collective-permute-start
  13.8 0.0 copy-done.10
  13.8 0.1 slice_convert_fusion.1
  13.9 0.0 copy-done.11
  13.9 0.2 reduce-window.8
  14.0 0.1 convert_reduce_fusion
  14.1 0.0 collective-permute-done.1
  14.2 0.1 fusion.2
  14.2 0.1 copy.11.weights_ref
  14.4 1.9 collective-permute-done.far_ref
  16.2 5.3 %shard_map.86 = f32[4736,128]{1,0:T(8,128)S(1)} custom-call(f32[512,512]{1,0:T(8,128)S(1)} %get-tuple-element.11.codes_ref, bf16[64,512]{1,0:T(8,128)(2,1)S(1)} %collective-permute-done.far_ref, f32[512,1]{1,0:T(8,128)S(1)} %copy.11.weights_ref), custom_call_target="tpu_custom_call" | custom-call | tf_op jit(solution)/shard_map/pallas_call | solution.py:407
  21.5 0.0 copy-start.1
  21.5 1.4 copy-done.1
  23.0 54.2 %shard_map.87 = f32[8,2,296,128]{3,2,1,0:T(8,128)S(1)} custom-call(f32[8,2,296,128]{3,2,1,0:T(8,128)} %bitcast.8), custom_call_target="tpu_custom_call" | custom-call | tf_op jit(solution)/shard_map/pallas_call | solution.py:409
  77.2 0.0 copy-start
  77.2 1.4 copy-done
  78.6 0.0 copy-start.3
  78.6 0.0 copy-start.9
  78.6 78.0 %shard_map.88 = (f32[1,512]{1,0:T(1,128)S(1)}, bf16[512,512]{1,0:T(8,128)(2,1)S(1)}, bf16[512,512]{1,0:T(8,128)(2,1)S(1)}) custom-call(f32[4736,128]{1,0:T(8,128)} %bitcast.7, f32[512,512]{1,0:T(8,128)S(1)} %get-tuple-element.11.codes_ref, bf16[64,512]{1,0:T(8,128)(2,1)S(1)} %collective-permute-done.far_ref, f32[512,1]{1,0:T(8,128)S(1)} %copy.11.weights_ref), custom_call_target="tpu_custom_call" | custom-call | tf_op jit(solution)/shard_map/pallas_call | solution.py:413
  156.6 0.0 copy-start.6
  156.6 0.8 copy-done.6
  157.4 0.0 copy-start.4
  157.4 0.8 copy-done.4
  158.2 2.3 %collective-permute-start.2 = (bf16[64,512]{1,0:T(8,128)(2,1)S(1)}, bf16[64,512]{1,0:T(8,128)(2,1)S(1)}, u32[]{:S(2)}, u32[]{:S(2)}) collective-permute-start(bf16[64,512]{1,0:T(8,128)(2,1)S(1)} %slice.17), channel_id=1, source_target_pairs={{0,1},{1,2},{2,3},{3,4},{4,5},{5,6},{6,7},{7,8},{8,9},{9,10},{10,1... | collective-permute-start | bytes 196616 | tf_op jit(solution)/shard_map/ppermute | solution.py:22
  160.5 0.6 reduce_sum.29
  161.1 0.3 collective-permute-done.2.back_ref
  161.4 0.0 copy-done.3
  161.4 0.0 copy-done.9
  161.4 0.0 copy-start.5
  161.4 1.0 copy-done.5
  162.4 0.0 copy-start.7
  162.4 1.0 copy-done.7
  163.5 11.1 %shard_map.89 = f32[16,768,128]{2,1,0:T(8,128)} custom-call(s32[8,8]{1,0:T(8,128)S(1)} %copy-done.9, bf16[512,4096]{1,0:T(8,128)(2,1)} %frames_ref.3, bf16[1024,512]{1,0:T(8,128)(2,1)S(1)} %copy-done.3, f32[512,1024]{1,0:T(8,128)} %get-tuple-element.13.squash_ref, bf16[512,1024]{1,0:T(8,128)(2,1)S(1)} %get-tuple-element.14.hidden_ref, ...), custom_call_target="tpu_custom_call" | custom-call | tf_op jit(solution)/shard_map/pallas_call | solution.py:422
  174.6 38.3 %shard_map.90 = (f32[512,128]{1,0:T(8,128)S(1)}, f32[64,512]{1,0:T(8,128)S(1)}) custom-call(f32[8,2,768,128]{3,2,1,0:T(8,128)} %bitcast.9), custom_call_target="tpu_custom_call" | custom-call | tf_op jit(solution)/shard_map/pallas_call | solution.py:425
  212.9 0.7 copy.15
  213.6 0.7 copy.16
  (5 shorter events, 0.0 us)
Async XLA Ops:
  1.3 12.8 %collective-permute-start.1 = (bf16[64]{0:T(256)(128)(2,1)S(1)}, bf16[64]{0:T(256)(128)(2,1)S(1)}, u32[]{:S(2)}, u32[]{:S(2)}) collective-permute-start(bf16[64]{0:T(256)(128)(2,1)S(1)} %slice.16), channel_id=1, source_target_pairs={{1,0},{2,1},{3,2},{4,3},{5,4},{6,5},{7,6},{8,7},{9,8},{10,9},{11,1... | collective-permute-start | bytes 392 | tf_op jit(solution)/shard_map/ppermute | solution.py:22
  2.6 1.2 copy-start.2
  3.8 0.7 copy-start.8
  4.5 9.3 %copy-start.10 = (s32[512]{0:T(512)S(1)}, s32[512]{0:T(512)}, u32[]{:S(2)}) copy-start(s32[512]{0:T(512)} %param.11) | copy-start | bytes 6148
  4.5 9.3 %copy-start.11 = (s32[4]{0:T(128)S(1)}, s32[4]{0:T(128)}, u32[]{:S(2)}) copy-start(s32[4]{0:T(128)} %param.6) | copy-start | bytes 52
  12.5 3.8 %collective-permute-start = (bf16[64,512]{1,0:T(8,128)(2,1)S(1)}, bf16[64,512]{1,0:T(8,128)(2,1)S(1)}, u32[]{:S(2)}, u32[]{:S(2)}) collective-permute-start(bf16[64,512]{1,0:T(8,128)(2,1)S(1)} %slice.21), channel_id=1, source_target_pairs={{1,0},{2,1},{3,2},{4,3},{5,4},{6,5},{7,6},{8,7},{9,8},{10,9},{11,1... | collective-permute-start | bytes 196616 | tf_op jit(solution)/shard_map/ppermute | solution.py:22
  21.5 1.4 copy-start.1
  77.2 1.4 copy-start
  78.6 82.8 %copy-start.3 = (bf16[1024,512]{1,0:T(8,128)(2,1)S(1)}, bf16[1024,512]{1,0:T(8,128)(2,1)}, u32[]{:S(2)}) copy-start(bf16[1024,512]{1,0:T(8,128)(2,1)} %second_ref.3) | copy-start | bytes 3145732
  78.6 82.8 %copy-start.9 = (s32[8,8]{1,0:T(8,128)S(1)}, s32[8,8]{1,0:T(8,128)}, u32[]{:S(2)}) copy-start(s32[8,8]{1,0:T(8,128)} %pattern_ref.3) | copy-start | bytes 772
  156.6 0.8 copy-start.6
  157.4 0.8 copy-start.4
  158.2 3.2 %collective-permute-start.2 = (bf16[64,512]{1,0:T(8,128)(2,1)S(1)}, bf16[64,512]{1,0:T(8,128)(2,1)S(1)}, u32[]{:S(2)}, u32[]{:S(2)}) collective-permute-start(bf16[64,512]{1,0:T(8,128)(2,1)S(1)} %slice.17), channel_id=1, source_target_pairs={{0,1},{1,2},{2,3},{3,4},{4,5},{5,6},{6,7},{7,8},{8,9},{9,10},{10,1... | collective-permute-start | bytes 196616 | tf_op jit(solution)/shard_map/ppermute | solution.py:22
  161.4 1.0 copy-start.5
  162.4 1.0 copy-start.7

commit v3 on v2

--- a/solution.py
+++ b/solution.py
@@ -10,6 +10,7 @@
 BLK = 128
 LAG = 64
 EPS = 0.01
+PIVOTS = 4
 HIGHEST = lax.Precision.HIGHEST
 VMEM = pl.BlockSpec(memory_space=pltpu.VMEM)
 SMEM = pl.BlockSpec(memory_space=pltpu.SMEM)
@@ -101,23 +102,42 @@
     out_ref[at + 2 * nb :, :] = jnp.broadcast_to(total, (spare, BLK))
 
 
+def eliminate(tiles, first, count):
+    lane = lax.broadcasted_iota(jnp.int32, (8, BLK), 1)
+    sub = lax.broadcasted_iota(jnp.int32, (8, BLK), 0)
+    span = range(count)
+    home, top = first // 8, first % 8
+    wide = lambda x: jnp.broadcast_to(x, (8, BLK))
+    rows = [wide(tiles[home][top + i : top + i + 1, :]) for i in span]
+    inv = [[wide(rows[i][:, first + j : first + j + 1]) for j in span] for i in span]
+    for k in span:
+        scale = 1.0 / inv[k][k]
+        row = [scale if j == k else inv[k][j] * scale for j in span]
+        inv = [
+            row if i == k else [-inv[i][k] * scale if j == k else inv[i][j] - inv[i][k] * row[j] for j in span]
+            for i in span
+        ]
+    fresh = []
+    for i in span:
+        row = sum(inv[i][j] * rows[j] for j in span)
+        for j in span:
+            row = jnp.where(lane == first + j, inv[i][j], row)
+        fresh.append(row)
+    inside = (lane >= first) & (lane < first + count)
+    out = []
+    for tile in tiles:
+        columns = [wide(tile[:, first + j : first + j + 1]) for j in span]
+        out.append(jnp.where(inside, 0.0, tile) - sum(columns[j] * fresh[j] for j in span))
+    for i in span:
+        out[home] = jnp.where(sub == top + i, fresh[i], out[home])
+    return out
+
+
 def invert_pair(one, two):
-    size = one.shape[0]
-    lane = lax.broadcasted_iota(jnp.int32, (size, size), 1)
-    sub = lax.broadcasted_iota(jnp.int32, (size, size), 0)
-    lane_row = lax.broadcasted_iota(jnp.int32, (1, size), 1)
-
-    def step(m, k):
-        column = m[:, k : k + 1]
-        row = m[k : k + 1, :]
-        inverse = 1.0 / m[k : k + 1, k : k + 1]
-        row = jnp.where(lane_row == k, inverse, row * inverse)
-        updated = jnp.where(lane == k, 0.0, m) - column * row
-        return jnp.where(sub == k, row, updated)
-
-    for k in range(size):
-        one, two = step(one, k), step(two, k)
-    return one, two
+    one, two = [[m[i : i + 8, :] for i in range(0, BLK, 8)] for m in (one, two)]
+    for first in range(0, BLK, PIVOTS):
+        one, two = eliminate(one, first, PIVOTS), eliminate(two, first, PIVOTS)
+    return jnp.concatenate(one, axis=0), jnp.concatenate(two, axis=0)
 
 
 def solve_kernel(stats_ref, codes_ref, far_ref, weights_ref, score_ref, cot_a_ref, cot_b_ref, inv_ref, cross_ref):
@@ -357,10 +377,14 @@
         second_ref[:, i * BLK : (i + 1) * BLK] = chunk_ref[top + i * tall : top + (i + 1) * tall, :]
 
 
-def exchanges_for(devices, rows, wire, align):
-    head = -(-(rows // 2) // align) * align
-    one, two = bit_orders(devices)
-    return [Exchange(devices, one, 0, head, wire), Exchange(devices, two, head, rows - head, wire)]
+def exchanges_for(devices, rows, wire, align, parts):
+    orders = bit_orders(devices)
+    units = rows // align
+    parts = min(parts, units)
+    ends = [align * (units * i // parts) for i in range(parts + 1)]
+    return [
+        Exchange(devices, orders[i % 2], ends[i], ends[i + 1] - ends[i], wire) for i in range(parts)
+    ]
 
 
 def exchange_call(kernel, exchanges, shapes, gather, ident, extra=()):
@@ -406,7 +430,7 @@
     per = -(-used // (8 * devices)) * 8
     (local_stats,) = call(moments_kernel, [((devices * per, BLK), f32)], [VMEM] * 3)(codes, far_codes, weights)
     halves = (devices // 2, 2, per, BLK)
-    (stats,) = exchange_call(reduce_kernel, exchanges_for(devices, per, f32, 8), [halves], True, 0)(
+    (stats,) = exchange_call(reduce_kernel, exchanges_for(devices, per, f32, 8, 4), [halves], True, 0)(
         local_stats.reshape(halves)
     )
     stats = stats.reshape(devices * per, BLK)
@@ -424,7 +448,7 @@
     )(pattern, frames, second_weight, squash, hidden, cot_a, cot_b, returned)
     share_first, share_second = exchange_call(
         scatter_kernel,
-        exchanges_for(devices, chunk, bf16, 16),
+        exchanges_for(devices, chunk, bf16, 16, 4),
         [(top, BLK), (tall, out)],
         False,
         1,

time: 215 us -> 183 us (0.85)
  Pallas kernels: 195 us -> 164 us
    pallas_call x1, Pallas kernels: 78 us -> 55.7 us  [body(): call(solve_kernel, [((1, out), f32), ((rows, out), bf16), ((rows, out), b...]
    pallas_call x2, Pallas kernels: 92.5 us -> 83.5 us  [the longest x1 49.7 us: body(): exchange_call(reduce_kernel, exchanges_for(devices, per, f32, 8, 4), [hal...]
where the time goes in v3:
time: 183 us
  Pallas kernels  164 us (90%)
  local copies, waits for them, and re-layouts  9.99 us (5%)
  starting transfers between devices  4.84 us (3%)
  waiting for transfers between devices  2.11 us (1%)
    pallas_call x1, Pallas kernels, body(): call(solve_kernel, [((1, out), f32), ((rows, out), bf16), ((rows, out), b...  55.7 us
    pallas_call x1, Pallas kernels, body(): exchange_call(reduce_kernel, exchanges_for(devices, per, f32, 8, 4), [hal...  49.7 us
    pallas_call x1, Pallas kernels, body(): exchange_call(scatter_kernel, exchanges_for(devices, chunk, bf16, 16, 4),...  33.8 us
    pallas_call x1, Pallas kernels, body(): call(backward_kernel, [((devices, chunk, BLK), f32)], [SMEM] + [VMEM] * 7...  11.1 us
    unnamed x26, local copies, waits for them, and re-layouts  9.83 us
    pallas_call x1, Pallas kernels, body(): call(encode_kernel, [((rows, hid), f32), ((rows, hid), bf16), ((rows, out...  7.94 us
    pallas_call x1, Pallas kernels, body(): call(moments_kernel, [((devices * per, BLK), f32)], [VMEM] * 3)  5.25 us
    ppermute x3, starting transfers between devices, from_behind(): return lax.ppermute(block, axis, route)  4.84 us
  transfers between devices with their start and end apart: 3, of which 2 were waited for; matrix products, arithmetic and copies ran while one was open for 1% of the time, Pallas kernels for 4%

profile of v3, /device:TPU:0, one launch (start us, length us, event | category | flops | bytes accessed | tf_op | source)
XLA Modules:
  0.0 182.9 jit_solution(4021197262281946532)
XLA Ops:
  0.6 0.7 convert.8
  1.3 1.3 collective-permute-start.1
  2.6 0.0 copy-start.2
  2.6 1.2 copy-done.2
  3.8 0.0 copy-start.8
  3.8 0.7 copy-done.8
  4.5 0.0 copy-start.10
  4.5 0.0 copy-start.11
  4.5 7.9 %shard_map.85 = (f32[512,1024]{1,0:T(8,128)}, bf16[512,1024]{1,0:T(8,128)(2,1)S(1)}, f32[512,512]{1,0:T(8,128)S(1)}) custom-call(s32[8,8]{1,0:T(8,128)S(1)} %copy-done.8, bf16[512,4096]{1,0:T(8,128)(2,1)} %frames_ref.3, bf16[8192,128]{1,0:T(8,128)(2,1)} %first_ref.1, bf16[1024,512]{1,0:T(8,128)(2,1)S(1)} %copy-done.2), custom_call_target="tpu_custom_call" | custom-call | tf_op jit(solution)/shard_map/pallas_call | solution.py:421
  12.5 1.3 collective-permute-start
  13.8 0.0 copy-done.10
  13.8 0.1 slice_convert_fusion.1
  13.9 0.0 copy-done.11
  13.9 0.2 reduce-window.8
  14.1 0.1 convert_reduce_fusion
  14.1 0.0 collective-permute-done.1
  14.2 0.1 fusion.2
  14.2 0.1 copy.11.weights_ref
  14.4 1.8 %collective-permute-done.far_ref = bf16[64,512]{1,0:T(8,128)(2,1)S(1)} collective-permute-done((bf16[64,512]{1,0:T(8,128)(2,1)S(1)}, bf16[64,512]{1,0:T(8,128)(2,1)S(1)}, u32[]{:S(2)}, u32[]{:S(2)}) %collective-permute-start) | collective-permute-done | bytes 65568 | tf_op jit(solution)/shard_map/ppermute | solution.py:23
  16.2 5.3 %shard_map.86 = f32[4736,128]{1,0:T(8,128)S(1)} custom-call(f32[512,512]{1,0:T(8,128)S(1)} %get-tuple-element.11.codes_ref, bf16[64,512]{1,0:T(8,128)(2,1)S(1)} %collective-permute-done.far_ref, f32[512,1]{1,0:T(8,128)S(1)} %copy.11.weights_ref), custom_call_target="tpu_custom_call" | custom-call | tf_op jit(solution)/shard_map/pallas_call | solution.py:431
  21.5 0.0 copy-start.1
  21.5 1.4 copy-done.1
  22.9 49.7 %shard_map.87 = f32[8,2,296,128]{3,2,1,0:T(8,128)S(1)} custom-call(f32[8,2,296,128]{3,2,1,0:T(8,128)} %bitcast.8), custom_call_target="tpu_custom_call" | custom-call | tf_op jit(solution)/shard_map/pallas_call | solution.py:433
  72.7 0.0 copy-start
  72.7 1.4 copy-done
  74.1 0.0 copy-start.3
  74.1 0.0 copy-start.9
  74.1 55.7 %shard_map.88 = (f32[1,512]{1,0:T(1,128)S(1)}, bf16[512,512]{1,0:T(8,128)(2,1)S(1)}, bf16[512,512]{1,0:T(8,128)(2,1)S(1)}) custom-call(f32[4736,128]{1,0:T(8,128)} %bitcast.7, f32[512,512]{1,0:T(8,128)S(1)} %get-tuple-element.11.codes_ref, bf16[64,512]{1,0:T(8,128)(2,1)S(1)} %collective-permute-done.far_ref, f32[512,1]{1,0:T(8,128)S(1)} %copy.11.weights_ref), custom_call_target="tpu_custom_call" | custom-call | tf_op jit(solution)/shard_map/pallas_call | solution.py:437
  129.8 0.0 copy-start.6
  129.8 0.8 copy-done.6
  130.6 0.0 copy-start.4
  130.6 0.8 copy-done.4
  131.4 2.3 %collective-permute-start.2 = (bf16[64,512]{1,0:T(8,128)(2,1)S(1)}, bf16[64,512]{1,0:T(8,128)(2,1)S(1)}, u32[]{:S(2)}, u32[]{:S(2)}) collective-permute-start(bf16[64,512]{1,0:T(8,128)(2,1)S(1)} %slice.17), channel_id=1, source_target_pairs={{0,1},{1,2},{2,3},{3,4},{4,5},{5,6},{6,7},{7,8},{8,9},{9,10},{10,1... | collective-permute-start | bytes 196616 | tf_op jit(solution)/shard_map/ppermute | solution.py:23
  133.7 0.6 reduce_sum.29
  134.3 0.3 collective-permute-done.2.back_ref
  134.6 0.0 copy-done.3
  134.6 0.0 copy-done.9
  134.6 0.0 copy-start.5
  134.6 1.0 copy-done.5
  135.6 0.0 copy-start.7
  135.6 1.0 copy-done.7
  136.7 11.1 %shard_map.89 = f32[16,768,128]{2,1,0:T(8,128)} custom-call(s32[8,8]{1,0:T(8,128)S(1)} %copy-done.9, bf16[512,4096]{1,0:T(8,128)(2,1)} %frames_ref.3, bf16[1024,512]{1,0:T(8,128)(2,1)S(1)} %copy-done.3, f32[512,1024]{1,0:T(8,128)} %get-tuple-element.13.squash_ref, bf16[512,1024]{1,0:T(8,128)(2,1)S(1)} %get-tuple-element.14.hidden_ref, ...), custom_call_target="tpu_custom_call" | custom-call | tf_op jit(solution)/shard_map/pallas_call | solution.py:446
  147.8 33.8 %shard_map.90 = (f32[512,128]{1,0:T(8,128)S(1)}, f32[64,512]{1,0:T(8,128)S(1)}) custom-call(f32[8,2,768,128]{3,2,1,0:T(8,128)} %bitcast.9), custom_call_target="tpu_custom_call" | custom-call | tf_op jit(solution)/shard_map/pallas_call | solution.py:449
  181.6 0.7 copy.15
  182.3 0.7 copy.16
  (5 shorter events, 0.0 us)
Async XLA Ops:
  1.3 12.8 %collective-permute-start.1 = (bf16[64]{0:T(256)(128)(2,1)S(1)}, bf16[64]{0:T(256)(128)(2,1)S(1)}, u32[]{:S(2)}, u32[]{:S(2)}) collective-permute-start(bf16[64]{0:T(256)(128)(2,1)S(1)} %slice.16), channel_id=1, source_target_pairs={{1,0},{2,1},{3,2},{4,3},{5,4},{6,5},{7,6},{8,7},{9,8},{10,9},{11,1... | collective-permute-start | bytes 392 | tf_op jit(solution)/shard_map/ppermute | solution.py:23
  2.6 1.2 copy-start.2
  3.8 0.7 copy-start.8
  4.5 9.3 %copy-start.10 = (s32[512]{0:T(512)S(1)}, s32[512]{0:T(512)}, u32[]{:S(2)}) copy-start(s32[512]{0:T(512)} %param.11) | copy-start | bytes 6148
  4.5 9.3 %copy-start.11 = (s32[4]{0:T(128)S(1)}, s32[4]{0:T(128)}, u32[]{:S(2)}) copy-start(s32[4]{0:T(128)} %param.6) | copy-start | bytes 52
  12.5 3.8 %collective-permute-start = (bf16[64,512]{1,0:T(8,128)(2,1)S(1)}, bf16[64,512]{1,0:T(8,128)(2,1)S(1)}, u32[]{:S(2)}, u32[]{:S(2)}) collective-permute-start(bf16[64,512]{1,0:T(8,128)(2,1)S(1)} %slice.21), channel_id=1, source_target_pairs={{1,0},{2,1},{3,2},{4,3},{5,4},{6,5},{7,6},{8,7},{9,8},{10,9},{11,1... | collective-permute-start | bytes 196616 | tf_op jit(solution)/shard_map/ppermute | solution.py:23
  21.5 1.4 copy-start.1
  72.7 1.4 copy-start
  74.1 60.5 %copy-start.3 = (bf16[1024,512]{1,0:T(8,128)(2,1)S(1)}, bf16[1024,512]{1,0:T(8,128)(2,1)}, u32[]{:S(2)}) copy-start(bf16[1024,512]{1,0:T(8,128)(2,1)} %second_ref.3) | copy-start | bytes 3145732
  74.1 60.5 %copy-start.9 = (s32[8,8]{1,0:T(8,128)S(1)}, s32[8,8]{1,0:T(8,128)}, u32[]{:S(2)}) copy-start(s32[8,8]{1,0:T(8,128)} %pattern_ref.3) | copy-start | bytes 772
  129.8 0.8 copy-start.6
  130.6 0.8 copy-start.4
  131.4 3.2 %collective-permute-start.2 = (bf16[64,512]{1,0:T(8,128)(2,1)S(1)}, bf16[64,512]{1,0:T(8,128)(2,1)S(1)}, u32[]{:S(2)}, u32[]{:S(2)}) collective-permute-start(bf16[64,512]{1,0:T(8,128)(2,1)S(1)} %slice.17), channel_id=1, source_target_pairs={{0,1},{1,2},{2,3},{3,4},{4,5},{5,6},{6,7},{7,8},{8,9},{9,10},{10,1... | collective-permute-start | bytes 196616 | tf_op jit(solution)/shard_map/ppermute | solution.py:23
  134.6 1.0 copy-start.5
  135.6 1.0 copy-start.7
